TPU v7x, 32 devices: a whole 2x2x4 slice. The times are simulated.
32 devices in a mesh: pipe: 2 (over x), expert: 16 (over z, y, core).
Axes of the slice: x: 2, y: 2, z: 4, core: 2. Of those that a mesh axis runs over, the one named last changes fastest.
Arguments:
- grad_out: bfloat16 [2, 2048, 2048], P('pipe', 'expert'), may hold values from -6 to 6
- expert_ids: int32 [2, 2048, 8], P('pipe', 'expert'), may hold values from 0 to 31, as said below
- slot_ids: int32 [2, 2048, 8], P('pipe', 'expert'), may hold values from 0 to 32, as said below
- gate_weights: float32 [2, 2048, 8], P('pipe', 'expert'), may hold values from 0.02 to 0.6
- saved_pre: bfloat16 [2, 32, 512, 1536], P('pipe', 'expert'), may hold values from -6 to 6
- down_weight: bfloat16 [2, 32, 768, 2048], P('pipe', 'expert'), may hold values from -0.21875 to 0.21875
- router_weight: bfloat16 [2, 32, 2048], P('pipe', 'expert'), may hold values from -0.125 to 0.125
Outputs:
- pre_grad: bfloat16 [2, 32, 512, 1536], P('pipe', 'expert')
- grad_inputs: bfloat16 [2, 2048, 2048], P('pipe', 'expert')
Inputs may be any that keep to these rules, and one draw needn't show every extreme that they name: `expert_ids`: each row names 8 different experts. `slot_ids`: for the pair (t, k): the number of earlier pairs (by row, then by k) among the same device's 128 rows of that section that name the same expert, capped at 32; the value 32 marks a pair that is dropped.
All inputs are finite; a program needn't handle non-finite values.
Results may differ from a plain program's by a relative error of at most 0.012.
Values may be sent and summed in bfloat16 or wider, within the bound.
A program may use at most 128 MiB of HBM per device.

v0:
```python
import jax
import jax.numpy as jnp
from jax import lax
from jax.sharding import PartitionSpec as P


def passed_along(value, axis, by):
    peers = lax.axis_size(axis)
    return lax.ppermute(value, axis, [(i, (i + by) % peers) for i in range(peers)])


def per_device(grad_out, expert_ids, slot_ids, gate_weights, saved_pre, down_weight, router_weight):
    groups = lax.axis_size("expert")
    local_experts = down_weight.shape[1]
    hidden_width = down_weight.shape[2]
    tok_rows = grad_out.shape[1]
    top_count = expert_ids.shape[2]
    expert_total = local_experts * groups
    capacity = tok_rows * top_count // expert_total
    total_rows = expert_total * capacity
    features = grad_out[0]
    route_ids = expert_ids[0]
    kept_pairs = slot_ids[0] < capacity
    destination = (
        route_ids % local_experts * (groups * capacity)
        + route_ids // local_experts * capacity
        + jnp.minimum(slot_ids[0], capacity - 1)
    )
    pair_dest = jnp.where(kept_pairs, destination, total_rows).reshape(-1)
    row_ids = jnp.arange(total_rows, dtype=jnp.int32)
    matches = pair_dest[None, :] == row_ids[:, None]
    pair_token = jnp.arange(tok_rows * top_count, dtype=jnp.int32) // top_count
    slot_token = jnp.sum(jnp.where(matches, pair_token[None, :], 0), axis=1)
    occupied = jnp.any(matches, axis=1)
    gate_low = gate_weights[0].astype(jnp.bfloat16)
    slot_gate = jnp.sum(
        jnp.where(matches, gate_low.reshape(-1).astype(jnp.float32)[None, :], jnp.float32(0.0)),
        axis=1,
    )
    token_rows = jnp.take(features, slot_token, axis=0)
    token_rows = jnp.where(occupied[:, None], token_rows, jnp.zeros_like(token_rows))
    pre_saved = saved_pre[0]
    gate_part = pre_saved[..., :hidden_width].astype(jnp.float32)
    up_part = pre_saved[..., hidden_width:].astype(jnp.float32)
    sigmoid_gate = jax.nn.sigmoid(gate_part)
    silu_gate = gate_part * sigmoid_gate
    hidden = (silu_gate * up_part).astype(jnp.bfloat16)
    weights = down_weight[0]
    expert_out = jnp.einsum(
        "jsf,jfd->jsd", hidden, weights, preferred_element_type=jnp.float32
    ).astype(jnp.bfloat16)
    scaled = (slot_gate[:, None] * token_rows.astype(jnp.float32)).astype(jnp.bfloat16)
    arrived = lax.all_to_all(
        scaled.reshape(local_experts, groups, capacity, -1),
        "expert",
        split_axis=1,
        concat_axis=1,
        tiled=True,
    )
    scaled_rows = arrived.reshape(local_experts, groups * capacity, -1)
    returned = lax.all_to_all(
        expert_out.reshape(local_experts, groups, capacity, -1),
        "expert",
        split_axis=1,
        concat_axis=1,
        tiled=True,
    )
    pair_out = jnp.take(
        returned.reshape(total_rows, -1), pair_dest, axis=0, mode="fill", fill_value=0
    )
    pair_scores = jnp.sum(
        pair_out.reshape(tok_rows, top_count, -1).astype(jnp.float32)
        * features.astype(jnp.float32)[:, None, :],
        axis=-1,
    )
    row_grad = jnp.einsum("jsd,jfd->jsf", scaled_rows, weights, preferred_element_type=jnp.float32)
    gate_grad = row_grad * up_part * sigmoid_gate * (1.0 + gate_part * (1.0 - sigmoid_gate))
    up_grad = row_grad * silu_gate
    pre_grad = jnp.concatenate([gate_grad, up_grad], axis=-1).astype(jnp.bfloat16)
    gate_values = gate_weights[0]
    weighted_sum = jnp.sum(gate_values * pair_scores, axis=-1, keepdims=True)
    select_grad = gate_values * (pair_scores - weighted_sum)
    expert_columns = jnp.arange(expert_total, dtype=jnp.int32)
    chosen = route_ids[:, :, None] == expert_columns[None, None, :]
    logit_grad = jnp.sum(
        jnp.where(chosen, select_grad[:, :, None], jnp.float32(0.0)), axis=1
    ).astype(jnp.bfloat16)
    router_part = jnp.dot(
        logit_grad,
        lax.all_gather(router_weight[0], "expert", axis=0, tiled=True),
        preferred_element_type=jnp.float32,
    )
    section_grad = (features.astype(jnp.float32) + router_part).astype(jnp.bfloat16)
    outgoing = passed_along(section_grad, "pipe", -1)
    return (pre_grad[None], outgoing[None])


def solution(mesh):
    in_specs = (
        P("pipe", "expert", None),
        P("pipe", "expert", None),
        P("pipe", "expert", None),
        P("pipe", "expert", None),
        P("pipe", "expert", None, None),
        P("pipe", "expert", None, None),
        P("pipe", "expert", None),
    )
    out_specs = (P("pipe", "expert", None, None), P("pipe", "expert", None))
    return jax.shard_map(
        per_device, mesh=mesh, in_specs=in_specs, out_specs=out_specs, check_vma=False
    )
```

profile of v0, /device:TPU:8, one launch (start us, length us, event | category | flops | bytes accessed | tf_op | source)
XLA Modules:
  0.0 253.1 jit_solution(6904118815322344028)
XLA Ops:
  0.6 7.4 %fusion.7 = bf16[2,512,2048]{2,1,0:T(8,128)(2,1)S(1)} fusion(bf16[1,2,768,2048]{3,2,1,0:T(8,128)(2,1)} %param.12, bf16[2,512,1536]{2,1,0:T(8,128)(2,1)} %bitcast.59), kind=kOutput, calls=%fused_computation.20 | convolution fusion | flops 3229614080 | bytes 13631488 | tf_op jit(solution)/shard_map/jsf,jfd->jsd/dot_general | solution.py:49
  8.0 2.3 copy.65
  10.3 6.4 %all-to-all-start.1 = ((bf16[2,16,32,2048]{3,2,0,1:T(8,128)(2,1)}), bf16[2,16,32,2048]{3,2,0,1:T(8,128)(2,1)}, u32[]{:S(2)}, u32[]{:S(2)}) async-start(bf16[2,16,32,2048]{3,2,0,1:T(8,128)(2,1)} %copy.65), calls=%async_computation.1 | async-start | bytes 8388608 | tf_op jit(solution)/shard_map/all_to_all | solution.py:61
  16.7 0.0 copy-done.1
  16.7 0.1 copy.55
  16.8 0.0 copy-done.3
  16.9 0.1 copy.54
  17.0 0.1 lt.78
  17.1 0.1 copy.56
  17.2 0.1 min.34
  17.3 0.1 squeeze.23
  17.4 0.5 select_reduce_fusion
  17.9 0.1 reduce_sum.53
  18.0 0.0 copy-done.2
  18.1 0.1 copy.57
  18.2 0.1 reshape.385
  18.2 0.5 select_reduce_fusion.1
  18.7 0.1 mul.113
  18.8 0.6 fusion.6
  19.4 0.1 broadcast_in_dim.95
  19.5 0.0 copy-done
  19.5 6.0 %gather_fusion = bf16[1024,2048]{1,0:T(8,128)(2,1)} fusion(bf16[128,2048]{1,0:T(8,128)(2,1)S(1)} %bitcast.49, s32[1024]{0:T(1024)S(1)} %broadcast_clamp_fusion.1), kind=kCustom, calls=%fused_computation | custom fusion | bytes 8392704 | tf_op jit(solution)/shard_map/jit(_take)/gather | solution.py:40
  25.6 4.5 %multiply_convert_fusion = bf16[2,16,32,2048]{3,2,0,1:T(8,128)(2,1)} fusion(bf16[2,16,32,2048]{3,2,1,0:T(8,128)(2,1)} %bitcast.51, f32[2,16,32]{2,0,1:T(2,128)S(1)} %copy.58, pred[2,16,32]{2,0,1:T(4,128)(4,1)S(1)} %copy.60, pred[2,16,32]{2,0,1:T(4,128)(4,1)S(1)} %copy.59), kind=kLoop, calls=%fused_computation.4 | loop fusion | flops 10485760 | bytes 8394752 | tf_op jit(solution)/shard_map/convert_element_type | solution.py:52
  30.1 77.5 %all-to-all-done.1 = bf16[2,16,32,2048]{3,2,0,1:T(8,128)(2,1)} async-done(((bf16[2,16,32,2048]{3,2,0,1:T(8,128)(2,1)}), bf16[2,16,32,2048]{3,2,0,1:T(8,128)(2,1)}, u32[]{:S(2)}, u32[]{:S(2)}) %all-to-all-start.1) | async-done | bytes 4194336 | tf_op jit(solution)/shard_map/all_to_all | solution.py:61
  107.6 6.6 %all-to-all-start = ((bf16[2,16,32,2048]{3,2,0,1:T(8,128)(2,1)}), bf16[2,16,32,2048]{3,2,0,1:T(8,128)(2,1)}, u32[]{:S(2)}, u32[]{:S(2)}) async-start(bf16[2,16,32,2048]{3,2,0,1:T(8,128)(2,1)} %multiply_convert_fusion), calls=%async_computation | async-start | bytes 8388608 | tf_op jit(solution)/shard_map/all_to_all | solution.py:53
  114.1 0.1 lt.85
  114.2 0.1 min.36
  114.3 0.1 squeeze.28
  114.4 0.1 copy.63
  114.5 0.1 copy.64
  114.6 0.1 broadcast_in_dim.103
  114.8 102.8 %all-gather = bf16[1,32,2048]{2,0,1:T(2,128)(2,1)S(1)} all-gather(bf16[1,2,2048]{2,0,1:T(2,128)(2,1)S(1)} %copy.71), channel_id=2, replica_groups=mesh['pipe'=2,'expert'=16] {'expert'}, dimensions={1}, use_global_device_ids=true | all-gather | bytes 139264 | tf_op jit(solution)/shard_map/all_gather | solution.py:90
  217.7 0.1 bitcast_convert_fusion
  217.8 4.7 %copy.66 = bf16[2,16,32,2048]{3,2,1,0:T(8,128)(2,1)} copy(bf16[2,16,32,2048]{3,2,0,1:T(8,128)(2,1)} %all-to-all-done.1) | data formatting | bytes 8388608 | tf_op jit(solution)/shard_map/all_to_all | solution.py:61
  222.5 11.6 %gather_fusion.1 = bf16[1024,2048]{1,0:T(8,128)(2,1)} fusion(bf16[1024,2048]{1,0:T(8,128)(2,1)} %bitcast.50, s32[1024]{0:T(1024)S(1)} %broadcast_clamp_fusion), kind=kCustom, calls=%fused_computation.1 | custom fusion | bytes 8392704 | tf_op jit(solution)/shard_map/jit(_take)/gather | solution.py:68
  234.1 3.2 %fusion = f32[1024]{0:T(1024)S(1)} fusion(f32[128,2048]{1,0:T(8,128)S(1)} %bitcast_convert_fusion, bf16[1024,2048]{1,0:T(8,128)(2,1)} %gather_fusion.1, pred[1024]{0:T(1024)(128)(4,1)S(1)} %broadcast_in_dim.103), kind=kLoop, calls=%fused_computation.3 | loop fusion | flops 8387584 | bytes 5248000 | tf_op jit(solution)/shard_map/reduce_sum | solution.py:71
  237.3 0.1 reduce_sum.56
  237.4 0.1 fusion.25
  237.5 0.1 bitcast_multiply_fusion.1
  237.7 0.3 fusion.18
  238.1 1.5 collective-permute-start
  239.6 0.0 all-to-all-done
  239.6 2.7 %copy.62 = bf16[2,16,32,2048]{3,2,1,0:T(8,128)(2,1)S(1)} copy(bf16[2,16,32,2048]{3,2,0,1:T(8,128)(2,1)} %all-to-all-done) | data formatting | bytes 8388608 | tf_op jit(solution)/shard_map/all_to_all | solution.py:53
  242.3 0.5 copy-done.5
  242.7 7.3 %fusion.21 = (bf16[1,2,512,768]{3,2,1,0:T(8,128)(2,1)S(1)}, bf16[1,2,512,768]{3,2,1,0:T(8,128)(2,1)S(1)}) fusion(bf16[2,512,1536]{2,1,0:T(8,128)(2,1)S(1)} %bitcast.60, bf16[2,512,2048]{2,1,0:T(8,128)(2,1)S(1)} %bitcast.52, bf16[1,2,768,2048]{3,2,1,0:T(8,128)(2,1)} %param.12), kind=kOutput, calls=%fused_computation.34 | convolution fusion | flops 3233021952 | bytes 16777216 | tf_op jit(solution)/shard_map/jsd,jfd->jsf/dot_general | solution.py:76
  250.0 1.9 pad_maximum_fusion
  251.9 0.4 collective-permute-done
  252.3 0.8 copy.83
  (22 shorter events, 0.3 us)
Async XLA Ops:
  10.3 6.5 %copy-start.1 = (s32[1,128,8]{1,2,0:T(8,128)S(1)}, s32[1,128,8]{1,2,0:T(8,128)}, u32[]{:S(2)}) copy-start(s32[1,128,8]{1,2,0:T(8,128)} %param.8) | copy-start | bytes 12292
  10.3 6.6 %copy-start.3 = (s32[1,128,8]{1,2,0:T(8,128)S(1)}, s32[1,128,8]{1,2,0:T(8,128)}, u32[]{:S(2)}) copy-start(s32[1,128,8]{1,2,0:T(8,128)} %param.9) | copy-start | bytes 12292
  10.3 7.7 %copy-start.2 = (f32[1,128,8]{1,2,0:T(8,128)S(1)}, f32[1,128,8]{1,2,0:T(8,128)}, u32[]{:S(2)}) copy-start(f32[1,128,8]{1,2,0:T(8,128)} %param.10) | copy-start | bytes 12292
  10.3 9.2 %copy-start = (bf16[1,128,2048]{2,1,0:T(8,128)(2,1)S(1)}, bf16[1,128,2048]{2,1,0:T(8,128)(2,1)}, u32[]{:S(2)}) copy-start(bf16[1,128,2048]{2,1,0:T(8,128)(2,1)} %param.7) | copy-start | bytes 1572868
  10.3 97.3 %all-to-all-start.1 = ((bf16[2,16,32,2048]{3,2,0,1:T(8,128)(2,1)}), bf16[2,16,32,2048]{3,2,0,1:T(8,128)(2,1)}, u32[]{:S(2)}, u32[]{:S(2)}) async-start(bf16[2,16,32,2048]{3,2,0,1:T(8,128)(2,1)} %copy.65), calls=%async_computation.1 | async-start | bytes 8388608 | tf_op jit(solution)/shard_map/all_to_all | solution.py:61
  30.1 84.7 %copy-start.4 = (bf16[1,2,2048]{2,1,0:T(2,128)(2,1)S(1)}, bf16[1,2,2048]{2,1,0:T(2,128)(2,1)}, u32[]{:S(2)}) copy-start(bf16[1,2,2048]{2,1,0:T(2,128)(2,1)} %param.13) | copy-start | bytes 24580
  107.6 132.0 %all-to-all-start = ((bf16[2,16,32,2048]{3,2,0,1:T(8,128)(2,1)}), bf16[2,16,32,2048]{3,2,0,1:T(8,128)(2,1)}, u32[]{:S(2)}, u32[]{:S(2)}) async-start(bf16[2,16,32,2048]{3,2,0,1:T(8,128)(2,1)} %multiply_convert_fusion), calls=%async_computation | async-start | bytes 8388608 | tf_op jit(solution)/shard_map/all_to_all | solution.py:53
  238.1 14.2 %collective-permute-start = (bf16[128,2048]{1,0:T(8,128)(2,1)S(1)}, bf16[128,2048]{1,0:T(8,128)(2,1)S(1)}, u32[]{:S(2)}, u32[]{:S(2)}) collective-permute-start(bf16[128,2048]{1,0:T(8,128)(2,1)S(1)} %fusion.18), channel_id=1, source_target_pairs={{0,16},{16,0},{1,17},{17,1},{2,18},{18,2},{3,19},{19,3},{4,20},{20... | collective-permute-start | bytes 1572872 | tf_op jit(solution)/shard_map/ppermute | solution.py:9
  239.6 3.2 %copy-start.5 = (bf16[1,2,512,1536]{3,2,1,0:T(8,128)(2,1)S(1)}, bf16[1,2,512,1536]{3,2,1,0:T(8,128)(2,1)}, u32[]{:S(2)}) copy-start(bf16[1,2,512,1536]{3,2,1,0:T(8,128)(2,1)} %param.11) | copy-start | bytes 9437188
where the time goes:
time: 253 us
  blocking collectives  103 us (41%)
  waiting for transfers between devices  77.8 us (31%)
  local copies, waits for them, and re-layouts  30.4 us (12%)
  matrix products  15 us (6%)
  starting transfers between devices  14.5 us (6%)
  other arithmetic  11.7 us (5%)
    all_gather x1, blocking collectives, per_device(): lax.all_gather(router_weight[0], 'expert', axis=0, tiled=True)  103 us
    all_to_all x1, waiting for transfers between devices, per_device(): lax.all_to_all(expert_out.reshape(local_experts, groups, capacity, -1), '...  77.5 us
    gather x1, local copies, waits for them, and re-layouts, per_device(): jnp.take(returned.reshape(total_rows, -1), pair_dest, axis=0, mode='fill'...  11.6 us
    dot_general x1, matrix products, per_device(): jnp.einsum('jsf,jfd->jsd', hidden, weights, preferred_element_type=jnp.fl...  7.37 us
    dot_general x1, matrix products, per_device(): jnp.einsum('jsd,jfd->jsf', scaled_rows, weights, preferred_element_type=j...  7.27 us
    all_to_all x1, starting transfers between devices, per_device(): lax.all_to_all(scaled.reshape(local_experts, groups, capacity, -1), 'expe...  6.55 us
    all_to_all x1, starting transfers between devices, per_device(): lax.all_to_all(expert_out.reshape(local_experts, groups, capacity, -1), '...  6.44 us
    gather x1, local copies, waits for them, and re-layouts, per_device(): token_rows = jnp.take(features, slot_token, axis=0)  6.02 us
  transfers between devices with their start and end apart: 3, of which 2 were waited for; matrix products, arithmetic and copies ran while one was open for 18% of the time, Pallas kernels for 0%

commit v1 on v0

v1 whole, which is shorter than its diff:
```python
import functools

import jax
import jax.numpy as jnp
from jax import lax
from jax.experimental import pallas as pl
from jax.experimental.pallas import tpu as pltpu
from jax.sharding import PartitionSpec as P

MESH = pl.DeviceIdType.MESH
LAYERS = 4
CHUNKS = 4
REPEAT = 8


def kernel(
    groups, pipes, cap,
    ids_ref, slots_ref, gates_ref, x_ref, router_ref, pre_ref, w_ref,
    out_ref, grad_ref,
    xbuf, wbuf, pbuf, fa, fs, sbuf, obuf, gbuf, nbuf, nids, ngates, rbuf, own_tab, tab, ts_out, ts_in, full_gate,
    local_sem, out_sem, x_send, x_recv, tab_send, tab_recv, near_send, near_recv, router_send, router_recv, ts_send, ts_recv,
):
    experts, width, features = w_ref.shape
    tok = x_ref.shape[0]
    top = ids_ref.shape[0]
    wide = groups // (2 * LAYERS)
    near_blocks = 2 * wide
    layer_rows = near_blocks * cap
    chunk = tok // CHUNKS
    tile = experts * REPEAT
    part = features // REPEAT

    pipe = lax.axis_index("pipe")
    me = lax.axis_index("expert")
    core = me % 2
    across = (me // 2) % wide
    layer = me // near_blocks
    before = (pipe + pipes - 1) % pipes
    after = (pipe + 1) % pipes
    sibling = layer * near_blocks + across * 2 + (1 - core)

    def other_layer(step):
        low = (layer % 2 + step % 2) % 2
        high = (layer // 2 + step // 2) % 2
        return high * 2 + low

    def block_of(at_layer, at_across, at_core):
        return at_layer * near_blocks + at_across * 2 + at_core

    load_x = pltpu.make_async_copy(x_ref, xbuf.at[me], local_sem.at[0])
    load_p = pltpu.make_async_copy(pre_ref, pbuf, local_sem.at[1])
    load_w = pltpu.make_async_copy(w_ref, wbuf, local_sem.at[2])
    load_x.start()
    load_p.start()
    load_w.start()

    barrier = pltpu.get_barrier_semaphore()

    def greet_peer(i, carry):
        pl.semaphore_signal(barrier, inc=1, device_id=(pipe, (me + i) % groups), device_id_type=MESH)
        return carry

    lax.fori_loop(1, groups, greet_peer, 0)

    def greet_before(i, carry):
        pl.semaphore_signal(barrier, inc=1, device_id=(before, (me + i) % groups), device_id_type=MESH)
        return carry

    lax.fori_loop(0, groups, greet_before, 0)
    greetings = 2 * groups - 1
    if pipes > 2:
        def greet_after(i, carry):
            pl.semaphore_signal(barrier, inc=1, device_id=(after, (me + i) % groups), device_id_type=MESH)
            return carry

        lax.fori_loop(0, groups, greet_after, 0)
        greetings += groups

    rows = lax.broadcasted_iota(jnp.int32, (groups * tile, tok), 0)
    row_expert = rows // REPEAT
    gate_acc = jnp.zeros((groups * tile, tok), jnp.float32)
    slot_acc = jnp.full((groups * tile, tok), -1.0, jnp.float32)
    for k in range(top):
        slot_k = slots_ref[k : k + 1, :]
        hit = (ids_ref[k : k + 1, :] == row_expert) & (slot_k < cap)
        low_k = gates_ref[k : k + 1, :].astype(jnp.bfloat16).astype(jnp.float32)
        gate_acc = jnp.where(hit, low_k, gate_acc)
        slot_acc = jnp.where(hit, slot_k.astype(jnp.float32), slot_acc)
    table = jnp.where(rows % REPEAT < REPEAT // 2, gate_acc, slot_acc)
    own_tab[...] = table.reshape(groups, tile, tok)

    pl.semaphore_wait(barrier, greetings)

    def x_copy(source, block, start, target):
        return pltpu.make_async_remote_copy(
            src_ref=source,
            dst_ref=xbuf.at[block, pl.ds(start, chunk)],
            send_sem=x_send.at[0],
            recv_sem=x_recv.at[block, start // chunk],
            device_id=(pipe, target),
            device_id_type=MESH,
        )

    for i in range(CHUNKS):
        source = x_ref.at[pl.ds(i * chunk, chunk)]
        for step in range(1, LAYERS):
            x_copy(source, me, i * chunk, block_of(other_layer(step), across, core)).start()
        for q in range(1, wide):
            x_copy(source, me, i * chunk, block_of(layer, (across + q) % wide, core)).start()
        x_copy(source, me, i * chunk, sibling).start()

    def send_table(i, carry):
        to = (me + i) % groups
        pltpu.make_async_remote_copy(
            src_ref=own_tab.at[to], dst_ref=tab.at[me], send_sem=tab_send.at[0], recv_sem=tab_recv.at[0],
            device_id=(pipe, to), device_id_type=MESH,
        ).start()
        return carry

    lax.fori_loop(1, groups, send_table, 0)
    tab[me] = own_tab[me]

    near = [
        pltpu.make_async_remote_copy(
            src_ref=source, dst_ref=target, send_sem=near_send.at[n], recv_sem=near_recv.at[n],
            device_id=(before, me), device_id_type=MESH,
        )
        for n, (source, target) in enumerate(((ids_ref, nids), (gates_ref, ngates), (x_ref, nbuf)))
    ]
    for copy in near:
        copy.start()

    def send_router(i, carry):
        to = (me + i) % groups
        pltpu.make_async_remote_copy(
            src_ref=router_ref, dst_ref=rbuf.at[me], send_sem=router_send.at[0], recv_sem=router_recv.at[0],
            device_id=(before, to), device_id_type=MESH,
        ).start()
        return carry

    lax.fori_loop(0, groups, send_router, 0)

    load_p.wait()
    step_rows = 64

    def factors(n, carry):
        at = pl.ds(pl.multiple_of(n * step_rows, step_rows), step_rows)
        for j in range(experts):
            a = pbuf[j, at, :width].astype(jnp.float32)
            b = pbuf[j, at, width:].astype(jnp.float32)
            s = jax.nn.sigmoid(a)
            fs[j, at, :] = a * s
            fa[j, at, :] = b * s * (1.0 + a * (1.0 - s))
        return carry

    lax.fori_loop(0, pbuf.shape[1] // step_rows, factors, 0)
    load_w.wait()
    load_x.wait()
    pltpu.make_async_copy(own_tab.at[pl.ds(0, groups - 1)], tab.at[pl.ds(0, groups - 1)], tab_recv.at[0]).wait()

    def arrived(block, start):
        view = xbuf.at[block, pl.ds(start, chunk)]
        pltpu.make_async_copy(view, view, x_recv.at[block, start // chunk]).wait()

    slot_rows = lax.broadcasted_iota(jnp.int32, (cap, tok), 0).astype(jnp.float32)

    def round_of(step, carry):
        here = other_layer(step)
        after_layer = other_layer(step + 1)

        def service(i, inner):
            start = pl.multiple_of(i * chunk, chunk)

            @pl.when(step < LAYERS - 1)
            def _():
                block = block_of(after_layer, across, core)
                arrived(block, start)
                view = xbuf.at[block, pl.ds(start, chunk)]
                for q in range(1, wide):
                    x_copy(view, block, start, block_of(layer, (across + q) % wide, core)).start()
                x_copy(view, block, start, sibling).start()

            for q in range(1, wide):
                block = block_of(here, (across + q) % wide, core)
                arrived(block, start)
                x_copy(xbuf.at[block, pl.ds(start, chunk)], block, start, sibling).start()
            return inner

        lax.fori_loop(0, CHUNKS, service, 0)

        def settle(i, inner):
            start = pl.multiple_of(i * chunk, chunk)
            for q in range(wide):
                arrived(block_of(here, q, 1 - core), start)
            return inner

        lax.fori_loop(0, CHUNKS, settle, 0)

        for n in range(near_blocks):
            block = here * near_blocks + n
            picks = []
            for j in range(experts):
                gate_row = tab[block, j * REPEAT : j * REPEAT + 1, :]
                slot_row = tab[block, j * REPEAT + REPEAT // 2 : j * REPEAT + REPEAT // 2 + 1, :]
                picks.append(jnp.where(slot_row == slot_rows, gate_row, 0.0).astype(jnp.bfloat16))
            picked = jnp.dot(
                jnp.concatenate(picks, axis=0), xbuf[block], preferred_element_type=jnp.float32
            ).astype(jnp.bfloat16)
            for j in range(experts):
                sbuf[j, n * cap : (n + 1) * cap, :] = picked[j * cap : (j + 1) * cap]

        at = pl.ds(pl.multiple_of(here * layer_rows, layer_rows), layer_rows)
        for j in range(experts):
            row_grad = lax.dot_general(
                sbuf[j], wbuf[j], (((1,), (1,)), ((), ())), preferred_element_type=jnp.float32
            )
            silu = fs[j, at, :]
            hidden = (silu * pbuf[j, at, width:].astype(jnp.float32)).astype(jnp.bfloat16).astype(jnp.float32)
            obuf[j, at, :width] = (row_grad * fa[j, at, :]).astype(jnp.bfloat16)
            obuf[j, at, width:] = (row_grad * silu).astype(jnp.bfloat16)
            score = jnp.sum(hidden * row_grad, axis=1, keepdims=True)
            for n in range(near_blocks):
                block = here * near_blocks + n
                slot_row = tab[block, j * REPEAT + REPEAT // 2 : j * REPEAT + REPEAT // 2 + 1, :]
                values = jnp.sum(
                    jnp.where(slot_row == slot_rows, score[n * cap : (n + 1) * cap], 0.0), axis=0, keepdims=True
                )
                ts_out[block, j * REPEAT : (j + 1) * REPEAT, :] = jnp.broadcast_to(values, (REPEAT, tok))
        for n in range(near_blocks):
            block = here * near_blocks + n
            pltpu.make_async_remote_copy(
                src_ref=ts_out.at[block], dst_ref=ts_in.at[me], send_sem=ts_send.at[0], recv_sem=ts_recv.at[0],
                device_id=(before, block), device_id_type=MESH,
            ).start()
        pltpu.make_async_copy(obuf.at[:, at, :], out_ref.at[:, at, :], out_sem.at[here]).start()
        return carry

    lax.fori_loop(0, LAYERS, round_of, 0)

    for copy in near:
        copy.wait_recv()
    gate = jnp.zeros((groups * tile, tok), jnp.float32)
    for k in range(top):
        gate = jnp.where(nids[k : k + 1, :] == row_expert, ngates[k : k + 1, :], gate)
    full_gate[...] = gate
    pltpu.make_async_copy(rbuf, rbuf, router_recv.at[0]).wait()
    pltpu.make_async_copy(ts_in, ts_in, ts_recv.at[0]).wait()
    gate = full_gate[...]
    gate_low = gate.astype(jnp.bfloat16).astype(jnp.float32)
    scaled_score = ts_in[...].reshape(groups * tile, tok)
    score = jnp.where(gate_low > 0.0, scaled_score / jnp.where(gate_low > 0.0, gate_low, 1.0), 0.0)
    total = jnp.sum(jnp.where(rows % REPEAT == 0, gate * score, 0.0), axis=0, keepdims=True)
    logit = jnp.transpose(gate * (score - total))
    lanes = lax.broadcasted_iota(jnp.int32, (tok, groups * tile), 1) % REPEAT
    router = rbuf[...].reshape(groups * tile, part)
    for d in range(REPEAT):
        left = jnp.where(lanes == d, logit, 0.0).astype(jnp.bfloat16)
        change = jnp.dot(left, router, preferred_element_type=jnp.float32)
        at = slice(d * part, (d + 1) * part)
        gbuf[:, at] = (nbuf[:, at].astype(jnp.float32) + change).astype(jnp.bfloat16)
    store = pltpu.make_async_copy(gbuf, grad_ref, local_sem.at[3])
    store.start()

    sent = xbuf.at[pl.ds(0, groups - 1)]
    pltpu.make_async_copy(sent, sent, x_send.at[0]).wait()
    pltpu.make_async_copy(own_tab.at[pl.ds(0, groups - 1)], tab.at[pl.ds(0, groups - 1)], tab_send.at[0]).wait()
    for copy in near:
        copy.wait_send()
    pltpu.make_async_copy(rbuf, rbuf, router_send.at[0]).wait()
    pltpu.make_async_copy(ts_in, ts_in, ts_send.at[0]).wait()
    for n in range(LAYERS):
        at = pl.ds(n * layer_rows, layer_rows)
        pltpu.make_async_copy(obuf.at[:, at, :], out_ref.at[:, at, :], out_sem.at[n]).wait()
    store.wait()


def per_device(grad_out, expert_ids, slot_ids, gate_weights, saved_pre, down_weight, router_weight):
    groups = lax.axis_size("expert")
    pipes = lax.axis_size("pipe")
    _, experts, width, features = down_weight.shape
    slots = saved_pre.shape[2]
    tok = grad_out.shape[1]
    top = expert_ids.shape[2]
    cap = slots // groups
    layer_rows = slots // LAYERS
    tile = experts * REPEAT
    part = features // REPEAT
    bf16, f32 = jnp.bfloat16, jnp.float32
    dma = pltpu.SemaphoreType.DMA
    vmem = pl.BlockSpec(memory_space=pltpu.VMEM)
    anywhere = pl.BlockSpec(memory_space=pl.ANY)
    pre_grad, grad_inputs = pl.pallas_call(
        functools.partial(kernel, groups, pipes, cap),
        out_shape=(
            jax.ShapeDtypeStruct((experts, slots, 2 * width), bf16),
            jax.ShapeDtypeStruct((tok, features), bf16),
        ),
        in_specs=[vmem, vmem, vmem, anywhere, vmem, anywhere, anywhere],
        out_specs=(anywhere, anywhere),
        scratch_shapes=[
            pltpu.VMEM((groups, tok, features), bf16),
            pltpu.VMEM((experts, width, features), bf16),
            pltpu.VMEM((experts, slots, 2 * width), bf16),
            pltpu.VMEM((experts, slots, width), f32),
            pltpu.VMEM((experts, slots, width), f32),
            pltpu.VMEM((experts, layer_rows, features), bf16),
            pltpu.VMEM((experts, slots, 2 * width), bf16),
            pltpu.VMEM((tok, features), bf16),
            pltpu.VMEM((tok, features), bf16),
            pltpu.VMEM((top, tok), jnp.int32),
            pltpu.VMEM((top, tok), f32),
            pltpu.VMEM((groups, tile, part), bf16),
            pltpu.VMEM((groups, tile, tok), f32),
            pltpu.VMEM((groups, tile, tok), f32),
            pltpu.VMEM((groups, tile, tok), f32),
            pltpu.VMEM((groups, tile, tok), f32),
            pltpu.VMEM((groups * tile, tok), f32),
            dma((4,)),
            dma((LAYERS,)),
            dma((1,)),
            dma((groups, CHUNKS)),
            dma((1,)),
            dma((1,)),
            dma((3,)),
            dma((3,)),
            dma((1,)),
            dma((1,)),
            dma((1,)),
            dma((1,)),
        ],
        compiler_params=pltpu.CompilerParams(
            collective_id=0, has_side_effects=True, vmem_limit_bytes=56 * 1024 * 1024
        ),
        cost_estimate=pl.CostEstimate(
            flops=2 * experts * slots * width * features, bytes_accessed=16 * 1024 * 1024, transcendentals=0
        ),
    )(
        expert_ids[0].T,
        slot_ids[0].T,
        gate_weights[0].T,
        grad_out[0],
        router_weight[0].reshape(tile, part),
        saved_pre[0],
        down_weight[0],
    )
    return (pre_grad[None], grad_inputs[None])


def solution(mesh):
    in_specs = (
        P("pipe", "expert", None),
        P("pipe", "expert", None),
        P("pipe", "expert", None),
        P("pipe", "expert", None),
        P("pipe", "expert", None, None),
        P("pipe", "expert", None, None),
        P("pipe", "expert", None),
    )
    out_specs = (P("pipe", "expert", None, None), P("pipe", "expert", None))
    return jax.shard_map(
        per_device, mesh=mesh, in_specs=in_specs, out_specs=out_specs, check_vma=False
    )
```

time: 253 us -> 113 us (0.45)
  the two profiles are of different devices: /device:TPU:8 before, /device:TPU:0 now
where the time goes in v1:
time: 113 us; the launch traced here: 112 us
  Pallas kernels  106 us (94%)
  local copies, waits for them, and re-layouts  5.92 us (5%)
    pallas_call x1, Pallas kernels, per_device(): pl.pallas_call(functools.partial(kernel, groups, pipes, cap), out_shape=(...  106 us
    unnamed x4, local copies, waits for them, and re-layouts  4.61 us

profile of v1, /device:TPU:0, one launch (start us, length us, event | category | flops | bytes accessed | tf_op | source)
XLA Modules:
  0.0 112.3 jit_solution(13409417790218056537)
XLA Ops:
  0.6 1.3 %reshape_squeeze.3.router_ref = bf16[16,256]{1,0:T(8,128)(2,1)} reshape(bf16[1,2,2048]{2,1,0:T(2,128)(2,1)} %param.13) | data formatting | bytes 16384 | tf_op jit(solution)/shard_map/reshape;squeeze | solution.py:342
  1.9 105.7 %shard_map.86 = (bf16[2,512,1536]{2,1,0:T(8,128)(2,1)}, bf16[128,2048]{1,0:T(8,128)(2,1)}) custom-call(s32[8,128]{1,0:T(8,128)} %bitcast.19, s32[8,128]{1,0:T(8,128)} %bitcast.20, f32[8,128]{1,0:T(8,128)} %bitcast.21, bf16[128,2048]{1,0:T(8,128)(2,1)} %bitcast.18, bf16[16,256]{1,0:T(8,128)(2,1)} %reshape_squeeze.3.router_ref, ...), custom_call_target="tpu_custom_call" | custom-call | flops 3221225472 | bytes 16777216 | tf_op jit(solution)/shard_map/pallas_call | solution.py:292
  107.6 0.0 copy-start
  107.6 3.8 %copy.11 = bf16[1,2,512,1536]{3,2,1,0:T(8,128)(2,1)} copy(bf16[1,2,512,1536]{3,2,1,0:T(8,128)(2,1)} %bitcast.14) | data formatting | bytes 6291456
  111.5 0.0 copy-done
  111.5 0.8 copy.12
Async XLA Ops:
  107.6 3.8 %copy-start = (bf16[128,2048]{1,0:T(8,128)(2,1)S(1)}, bf16[128,2048]{1,0:T(8,128)(2,1)}, u32[]{:S(2)}) copy-start(bf16[128,2048]{1,0:T(8,128)(2,1)} %get-tuple-element.5) | copy-start | bytes 1572868

commit v2 on v1

--- a/solution.py
+++ b/solution.py
@@ -9,16 +9,18 @@
 
 MESH = pl.DeviceIdType.MESH
 LAYERS = 4
-CHUNKS = 4
+CHUNKS = 8
+PARTS = 3
 REPEAT = 8
+UP, SIDE_UP, OWN_SIDE, SIDE, SIB = 0, 2, 4, 5, 6
 
 
 def kernel(
     groups, pipes, cap,
     ids_ref, slots_ref, gates_ref, x_ref, router_ref, pre_ref, w_ref,
     out_ref, grad_ref,
-    xbuf, wbuf, pbuf, fa, fs, sbuf, obuf, gbuf, nbuf, nids, ngates, rbuf, own_tab, tab, ts_out, ts_in, full_gate,
-    local_sem, out_sem, x_send, x_recv, tab_send, tab_recv, near_send, near_recv, router_send, router_recv, ts_send, ts_recv,
+    xbuf, wbuf, pbuf, fa, fs, sbuf, obuf, gbuf, nbuf, nids, ngates, rbuf, own_tab, tab, ts_out, ts_in, full_gate, scores,
+    local_sem, out_sem, x_send, x_recv, sib_recv, tab_send, tab_recv, near_send, near_recv, router_send, router_recv, ts_send, ts_recv,
 ):
     experts, width, features = w_ref.shape
     tok = x_ref.shape[0]
@@ -39,13 +41,17 @@
     after = (pipe + 1) % pipes
     sibling = layer * near_blocks + across * 2 + (1 - core)
 
-    def other_layer(step):
-        low = (layer % 2 + step % 2) % 2
-        high = (layer // 2 + step // 2) % 2
-        return high * 2 + low
-
     def block_of(at_layer, at_across, at_core):
         return at_layer * near_blocks + at_across * 2 + at_core
+
+    inner_layer = ((layer + 1) // 2) % 2
+    flip = layer // 2
+
+    def order(p):
+        base = (1 - inner_layer) * p + inner_layer * ((p + 1) % 3 + 2 * (p // 3))
+        first = (1 - (p + LAYERS - 1) // LAYERS) * layer
+        other = (1 - flip) * base + flip * (LAYERS - 1 - base)
+        return first + ((p + LAYERS - 1) // LAYERS) * other
 
     load_x = pltpu.make_async_copy(x_ref, xbuf.at[me], local_sem.at[0])
     load_p = pltpu.make_async_copy(pre_ref, pbuf, local_sem.at[1])
@@ -91,23 +97,43 @@
 
     pl.semaphore_wait(barrier, greetings)
 
-    def x_copy(source, block, start, target):
+    def x_copy(source, block, start, target, sent, arrives):
         return pltpu.make_async_remote_copy(
             src_ref=source,
             dst_ref=xbuf.at[block, pl.ds(start, chunk)],
-            send_sem=x_send.at[0],
-            recv_sem=x_recv.at[block, start // chunk],
+            send_sem=x_send.at[sent],
+            recv_sem=arrives,
             device_id=(pipe, target),
             device_id_type=MESH,
         )
 
+    def along(source, block, start, up, down, sent):
+        arrives = x_recv.at[block, start // chunk]
+
+        @pl.when(up * (LAYERS - 1 - layer) > 0)
+        def _():
+            x_copy(source, block, start, me + near_blocks, sent, arrives).start()
+
+        @pl.when(down * layer > 0)
+        def _():
+            x_copy(source, block, start, me - near_blocks, sent + 1, arrives).start()
+
+    def sideways(source, block, start, sent):
+        arrives = x_recv.at[block, start // chunk]
+        for q in range(1, wide):
+            x_copy(source, block, start, block_of(layer, (across + q) % wide, core), sent, arrives).start()
+
+    def over(source, block, start):
+        x_copy(source, block, start, sibling, SIB, sib_recv.at[block]).start()
+
+    last = (CHUNKS - 1) * chunk
+    sideways(x_ref.at[pl.ds(last, chunk)], me, last, OWN_SIDE)
     for i in range(CHUNKS):
         source = x_ref.at[pl.ds(i * chunk, chunk)]
-        for step in range(1, LAYERS):
-            x_copy(source, me, i * chunk, block_of(other_layer(step), across, core)).start()
-        for q in range(1, wide):
-            x_copy(source, me, i * chunk, block_of(layer, (across + q) % wide, core)).start()
-        x_copy(source, me, i * chunk, sibling).start()
+        along(source, me, i * chunk, 1, 1, UP)
+        if i < CHUNKS - 1:
+            sideways(source, me, i * chunk, OWN_SIDE)
+        over(source, me, i * chunk)
 
     def send_table(i, carry):
         to = (me + i) % groups
@@ -164,78 +190,120 @@
 
     slot_rows = lax.broadcasted_iota(jnp.int32, (cap, tok), 0).astype(jnp.float32)
 
-    def round_of(step, carry):
-        here = other_layer(step)
-        after_layer = other_layer(step + 1)
-
-        def service(i, inner):
+    pick_blocks = near_blocks // 4
+    part_width = width // PARTS
+
+    def round_of(p, carry):
+        here = order(p % LAYERS)
+        coming = order((p + 1) % LAYERS)
+        ready = order((p + LAYERS - 1) % LAYERS)
+        at = pl.ds(pl.multiple_of(ready * layer_rows, layer_rows), layer_rows)
+        up = (LAYERS - 1 + layer - coming) // LAYERS
+        down = (LAYERS - 1 + coming - layer) // LAYERS
+
+        @pl.when(p > 0)
+        def _():
+            for q in range(wide):
+                view = xbuf.at[block_of(ready, q, 1 - core)]
+                pltpu.make_async_copy(view, view, sib_recv.at[block_of(ready, q, 1 - core)]).wait()
+
+        def step(i, inner):
             start = pl.multiple_of(i * chunk, chunk)
 
-            @pl.when(step < LAYERS - 1)
+            @pl.when(p < LAYERS - 1)
             def _():
-                block = block_of(after_layer, across, core)
+                block = block_of(coming, across, core)
                 arrived(block, start)
                 view = xbuf.at[block, pl.ds(start, chunk)]
+                along(view, block, start, up, down, UP)
+
+                @pl.when(i < CHUNKS - 1)
+                def _():
+                    sideways(view, block, start, SIDE)
+
+                over(view, block, start)
+
+                @pl.when(i == CHUNKS - 1)
+                def _():
+                    for q in range(1, wide):
+                        block = block_of(coming, (across + q) % wide, core)
+                        arrived(block, last)
+                        view = xbuf.at[block, pl.ds(last, chunk)]
+                        along(view, block, last, up, down, SIDE_UP)
+                        over(view, block, last)
+
+            @pl.when((p < LAYERS) & (i < CHUNKS - 1))
+            def _():
                 for q in range(1, wide):
-                    x_copy(view, block, start, block_of(layer, (across + q) % wide, core)).start()
-                x_copy(view, block, start, sibling).start()
-
-            for q in range(1, wide):
-                block = block_of(here, (across + q) % wide, core)
-                arrived(block, start)
-                x_copy(xbuf.at[block, pl.ds(start, chunk)], block, start, sibling).start()
+                    block = block_of(here, (across + q) % wide, core)
+                    arrived(block, start)
+                    over(xbuf.at[block, pl.ds(start, chunk)], block, start)
+
+            @pl.when((p == 0) & (i == 0))
+            def _():
+                for q in range(1, wide):
+                    block = block_of(layer, (across + q) % wide, core)
+                    arrived(block, last)
+                    view = xbuf.at[block, pl.ds(last, chunk)]
+                    along(view, block, last, 1, 1, SIDE_UP)
+                    over(view, block, last)
+
+            @pl.when((p > 0) & (i < 4))
+            def _():
+                for n in range(pick_blocks):
+                    block = ready * near_blocks + i * pick_blocks + n
+                    picks = []
+                    for j in range(experts):
+                        gate_row = tab[block, j * REPEAT : j * REPEAT + 1, :]
+                        slot_row = tab[block, j * REPEAT + REPEAT // 2 : j * REPEAT + REPEAT // 2 + 1, :]
+                        picks.append(jnp.where(slot_row == slot_rows, gate_row, 0.0).astype(jnp.bfloat16))
+                    picked = jnp.dot(
+                        jnp.concatenate(picks, axis=0), xbuf[block], preferred_element_type=jnp.float32
+                    ).astype(jnp.bfloat16)
+                    to = pl.ds(pl.multiple_of((i * pick_blocks + n) * cap, cap), cap)
+                    for j in range(experts):
+                        sbuf[j, to, :] = picked[j * cap : (j + 1) * cap]
+
+            for m in range(PARTS):
+                @pl.when((p > 0) & (i == 4 + m))
+                def _():
+                    left = slice(m * part_width, (m + 1) * part_width)
+                    right = slice(width + m * part_width, width + (m + 1) * part_width)
+                    for j in range(experts):
+                        row_grad = lax.dot_general(
+                            sbuf[j], wbuf[j, left], (((1,), (1,)), ((), ())), preferred_element_type=jnp.float32
+                        )
+                        silu = fs[j, at, left]
+                        hidden = (silu * pbuf[j, at, right].astype(jnp.float32)).astype(jnp.bfloat16)
+                        obuf[j, at, left] = (row_grad * fa[j, at, left]).astype(jnp.bfloat16)
+                        obuf[j, at, right] = (row_grad * silu).astype(jnp.bfloat16)
+                        score = jnp.sum(hidden.astype(jnp.float32) * row_grad, axis=1, keepdims=True)
+                        score = jnp.broadcast_to(score, (layer_rows, tok))
+                        scores[j] = score if m == 0 else scores[j] + score
+
+            @pl.when((p > 0) & (i == 4 + PARTS))
+            def _():
+                for n in range(near_blocks):
+                    block = ready * near_blocks + n
+                    for j in range(experts):
+                        slot_row = tab[block, j * REPEAT + REPEAT // 2 : j * REPEAT + REPEAT // 2 + 1, :]
+                        values = jnp.sum(
+                            jnp.where(slot_row == slot_rows, scores[j, n * cap : (n + 1) * cap, :], 0.0),
+                            axis=0,
+                            keepdims=True,
+                        )
+                        ts_out[block, j * REPEAT : (j + 1) * REPEAT, :] = jnp.broadcast_to(values, (REPEAT, tok))
+                    pltpu.make_async_remote_copy(
+                        src_ref=ts_out.at[block], dst_ref=ts_in.at[me], send_sem=ts_send.at[0], recv_sem=ts_recv.at[0],
+                        device_id=(before, block), device_id_type=MESH,
+                    ).start()
+                pltpu.make_async_copy(obuf.at[:, at, :], out_ref.at[:, at, :], out_sem.at[ready]).start()
             return inner
 
-        lax.fori_loop(0, CHUNKS, service, 0)
-
-        def settle(i, inner):
-            start = pl.multiple_of(i * chunk, chunk)
-            for q in range(wide):
-                arrived(block_of(here, q, 1 - core), start)
-            return inner
-
-        lax.fori_loop(0, CHUNKS, settle, 0)
-
-        for n in range(near_blocks):
-            block = here * near_blocks + n
-            picks = []
-            for j in range(experts):
-                gate_row = tab[block, j * REPEAT : j * REPEAT + 1, :]
-                slot_row = tab[block, j * REPEAT + REPEAT // 2 : j * REPEAT + REPEAT // 2 + 1, :]
-                picks.append(jnp.where(slot_row == slot_rows, gate_row, 0.0).astype(jnp.bfloat16))
-            picked = jnp.dot(
-                jnp.concatenate(picks, axis=0), xbuf[block], preferred_element_type=jnp.float32
-            ).astype(jnp.bfloat16)
-            for j in range(experts):
-                sbuf[j, n * cap : (n + 1) * cap, :] = picked[j * cap : (j + 1) * cap]
-
-        at = pl.ds(pl.multiple_of(here * layer_rows, layer_rows), layer_rows)
-        for j in range(experts):
-            row_grad = lax.dot_general(
-                sbuf[j], wbuf[j], (((1,), (1,)), ((), ())), preferred_element_type=jnp.float32
-            )
-            silu = fs[j, at, :]
-            hidden = (silu * pbuf[j, at, width:].astype(jnp.float32)).astype(jnp.bfloat16).astype(jnp.float32)
-            obuf[j, at, :width] = (row_grad * fa[j, at, :]).astype(jnp.bfloat16)
-            obuf[j, at, width:] = (row_grad * silu).astype(jnp.bfloat16)
-            score = jnp.sum(hidden * row_grad, axis=1, keepdims=True)
-            for n in range(near_blocks):
-                block = here * near_blocks + n
-                slot_row = tab[block, j * REPEAT + REPEAT // 2 : j * REPEAT + REPEAT // 2 + 1, :]
-                values = jnp.sum(
-                    jnp.where(slot_row == slot_rows, score[n * cap : (n + 1) * cap], 0.0), axis=0, keepdims=True
-                )
-                ts_out[block, j * REPEAT : (j + 1) * REPEAT, :] = jnp.broadcast_to(values, (REPEAT, tok))
-        for n in range(near_blocks):
-            block = here * near_blocks + n
-            pltpu.make_async_remote_copy(
-                src_ref=ts_out.at[block], dst_ref=ts_in.at[me], send_sem=ts_send.at[0], recv_sem=ts_recv.at[0],
-                device_id=(before, block), device_id_type=MESH,
-            ).start()
-        pltpu.make_async_copy(obuf.at[:, at, :], out_ref.at[:, at, :], out_sem.at[here]).start()
-        return carry
-
-    lax.fori_loop(0, LAYERS, round_of, 0)
+        lax.fori_loop(0, CHUNKS, step, 0)
+        return carry
+
+    lax.fori_loop(0, LAYERS + 1, round_of, 0)
 
     for copy in near:
         copy.wait_recv()
@@ -261,8 +329,25 @@
     store = pltpu.make_async_copy(gbuf, grad_ref, local_sem.at[3])
     store.start()
 
-    sent = xbuf.at[pl.ds(0, groups - 1)]
-    pltpu.make_async_copy(sent, sent, x_send.at[0]).wait()
+    def all_sent(blocks, count, sem):
+        view = xbuf.at[pl.ds(0, blocks), pl.ds(0, count)]
+        pltpu.make_async_copy(view, view, x_send.at[sem]).wait()
+
+    all_sent(groups // 2, tok, SIB)
+    if wide > 1:
+        all_sent(wide - 1, tok, OWN_SIDE)
+        all_sent((LAYERS - 1) * (wide - 1), tok - chunk, SIDE)
+    for n in range(LAYERS):
+        @pl.when(layer == n)
+        def _():
+            if n < LAYERS - 1:
+                all_sent(n + 1, tok, UP)
+                if wide > 1:
+                    all_sent((n + 1) * (wide - 1), chunk, SIDE_UP)
+            if n > 0:
+                all_sent(LAYERS - n, tok, UP + 1)
+                if wide > 1:
+                    all_sent((LAYERS - n) * (wide - 1), chunk, SIDE_UP + 1)
     pltpu.make_async_copy(own_tab.at[pl.ds(0, groups - 1)], tab.at[pl.ds(0, groups - 1)], tab_send.at[0]).wait()
     for copy in near:
         copy.wait_send()
@@ -315,10 +400,12 @@
             pltpu.VMEM((groups, tile, tok), f32),
             pltpu.VMEM((groups, tile, tok), f32),
             pltpu.VMEM((groups * tile, tok), f32),
+            pltpu.VMEM((experts, layer_rows, tok), f32),
             dma((4,)),
             dma((LAYERS,)),
-            dma((1,)),
+            dma((7,)),
             dma((groups, CHUNKS)),
+            dma((groups,)),
             dma((1,)),
             dma((1,)),
             dma((3,)),

time: 113 us -> 75.7 us (0.67)
  Pallas kernels: 106 us -> 68.9 us
    pallas_call x1, Pallas kernels: 106 us -> 68.9 us  [per_device(): pl.pallas_call(functools.partial(kernel, groups, pipes, cap), out_shape=(...]
where the time goes in v2:
time: 75.7 us; the launch traced here: 75.4 us
  Pallas kernels  68.9 us (91%)
  local copies, waits for them, and re-layouts  5.92 us (8%)
    pallas_call x1, Pallas kernels, per_device(): pl.pallas_call(functools.partial(kernel, groups, pipes, cap), out_shape=(...  68.9 us
    unnamed x4, local copies, waits for them, and re-layouts  4.61 us

profile of v2, /device:TPU:0, one launch (start us, length us, event | category | flops | bytes accessed | tf_op | source)
XLA Modules:
  0.0 75.4 jit_solution(15163036277526176693)
XLA Ops:
  0.6 1.3 %reshape_squeeze.3.router_ref = bf16[16,256]{1,0:T(8,128)(2,1)} reshape(bf16[1,2,2048]{2,1,0:T(2,128)(2,1)} %param.13) | data formatting | bytes 16384 | tf_op jit(solution)/shard_map/reshape;squeeze | solution.py:429
  1.9 68.9 %shard_map.86 = (bf16[2,512,1536]{2,1,0:T(8,128)(2,1)}, bf16[128,2048]{1,0:T(8,128)(2,1)}) custom-call(s32[8,128]{1,0:T(8,128)} %bitcast.19, s32[8,128]{1,0:T(8,128)} %bitcast.20, f32[8,128]{1,0:T(8,128)} %bitcast.21, bf16[128,2048]{1,0:T(8,128)(2,1)} %bitcast.18, bf16[16,256]{1,0:T(8,128)(2,1)} %reshape_squeeze.3.router_ref, ...), custom_call_target="tpu_custom_call" | custom-call | flops 3221225472 | bytes 16777216 | tf_op jit(solution)/shard_map/pallas_call | solution.py:377
  70.8 0.0 copy-start
  70.8 3.8 %copy.11 = bf16[1,2,512,1536]{3,2,1,0:T(8,128)(2,1)} copy(bf16[1,2,512,1536]{3,2,1,0:T(8,128)(2,1)} %bitcast.14) | data formatting | bytes 6291456
  74.6 0.0 copy-done
  74.6 0.8 %copy.12 = bf16[1,128,2048]{2,1,0:T(8,128)(2,1)} copy(bf16[1,128,2048]{2,1,0:T(8,128)(2,1)S(1)} %bitcast.15) | data formatting | bytes 1048576
Async XLA Ops:
  70.8 3.8 %copy-start = (bf16[128,2048]{1,0:T(8,128)(2,1)S(1)}, bf16[128,2048]{1,0:T(8,128)(2,1)}, u32[]{:S(2)}) copy-start(bf16[128,2048]{1,0:T(8,128)(2,1)} %get-tuple-element.5) | copy-start | bytes 1572868

commit v3 on v2

--- a/solution.py
+++ b/solution.py
@@ -19,7 +19,7 @@
     groups, pipes, cap,
     ids_ref, slots_ref, gates_ref, x_ref, router_ref, pre_ref, w_ref,
     out_ref, grad_ref,
-    xbuf, wbuf, pbuf, fa, fs, sbuf, obuf, gbuf, nbuf, nids, ngates, rbuf, own_tab, tab, ts_out, ts_in, full_gate, scores,
+    xbuf, wbuf, pbuf, fa, fs, sbuf, obuf, gbuf, nbuf, nids, ngates, rbuf, own_tab, tab, ts_out, ts_in, full_gate, scores, router_own,
     local_sem, out_sem, x_send, x_recv, sib_recv, tab_send, tab_recv, near_send, near_recv, router_send, router_recv, ts_send, ts_recv,
 ):
     experts, width, features = w_ref.shape
@@ -95,6 +95,11 @@
     table = jnp.where(rows % REPEAT < REPEAT // 2, gate_acc, slot_acc)
     own_tab[...] = table.reshape(groups, tile, tok)
 
+    router_rows = router_ref[...].astype(jnp.float32)
+    router_own[...] = jnp.concatenate(
+        [router_rows[j : j + 1, d * part : (d + 1) * part] for j in range(experts) for d in range(REPEAT)], axis=0
+    ).astype(jnp.bfloat16)
+
     pl.semaphore_wait(barrier, greetings)
 
     def x_copy(source, block, start, target, sent, arrives):
@@ -159,7 +164,7 @@
     def send_router(i, carry):
         to = (me + i) % groups
         pltpu.make_async_remote_copy(
-            src_ref=router_ref, dst_ref=rbuf.at[me], send_sem=router_send.at[0], recv_sem=router_recv.at[0],
+            src_ref=router_own, dst_ref=rbuf.at[me], send_sem=router_send.at[0], recv_sem=router_recv.at[0],
             device_id=(before, to), device_id_type=MESH,
         ).start()
         return carry
@@ -167,22 +172,16 @@
     lax.fori_loop(0, groups, send_router, 0)
 
     load_p.wait()
-    step_rows = 64
-
-    def factors(n, carry):
-        at = pl.ds(pl.multiple_of(n * step_rows, step_rows), step_rows)
+    factor_rows = pbuf.shape[1] // CHUNKS
+
+    def factors(n):
+        at = pl.ds(pl.multiple_of(n * factor_rows, factor_rows), factor_rows)
         for j in range(experts):
             a = pbuf[j, at, :width].astype(jnp.float32)
             b = pbuf[j, at, width:].astype(jnp.float32)
             s = jax.nn.sigmoid(a)
             fs[j, at, :] = a * s
             fa[j, at, :] = b * s * (1.0 + a * (1.0 - s))
-        return carry
-
-    lax.fori_loop(0, pbuf.shape[1] // step_rows, factors, 0)
-    load_w.wait()
-    load_x.wait()
-    pltpu.make_async_copy(own_tab.at[pl.ds(0, groups - 1)], tab.at[pl.ds(0, groups - 1)], tab_recv.at[0]).wait()
 
     def arrived(block, start):
         view = xbuf.at[block, pl.ds(start, chunk)]
@@ -200,6 +199,14 @@
         at = pl.ds(pl.multiple_of(ready * layer_rows, layer_rows), layer_rows)
         up = (LAYERS - 1 + layer - coming) // LAYERS
         down = (LAYERS - 1 + coming - layer) // LAYERS
+
+        @pl.when(p == 1)
+        def _():
+            load_w.wait()
+            load_x.wait()
+            pltpu.make_async_copy(
+                own_tab.at[pl.ds(0, groups - 1)], tab.at[pl.ds(0, groups - 1)], tab_recv.at[0]
+            ).wait()
 
         @pl.when(p > 0)
         def _():
@@ -247,6 +254,10 @@
                     view = xbuf.at[block, pl.ds(last, chunk)]
                     along(view, block, last, 1, 1, SIDE_UP)
                     over(view, block, last)
+
+            @pl.when(p == 0)
+            def _():
+                factors(i)
 
             @pl.when((p > 0) & (i < 4))
             def _():
@@ -401,6 +412,7 @@
             pltpu.VMEM((groups, tile, tok), f32),
             pltpu.VMEM((groups * tile, tok), f32),
             pltpu.VMEM((experts, layer_rows, tok), f32),
+            pltpu.VMEM((tile, part), bf16),
             dma((4,)),
             dma((LAYERS,)),
             dma((7,)),
@@ -426,7 +438,7 @@
         slot_ids[0].T,
         gate_weights[0].T,
         grad_out[0],
-        router_weight[0].reshape(tile, part),
+        router_weight[0],
         saved_pre[0],
         down_weight[0],
     )

time: 75.7 us -> 72 us (0.951)
  Pallas kernels: 68.9 us -> 66.5 us
  local copies, waits for them, and re-layouts: 5.92 us -> 4.61 us
    pallas_call x1, Pallas kernels: 68.9 us -> 66.5 us  [per_device(): pl.pallas_call(functools.partial(kernel, groups, pipes, cap), out_shape=(...]
    another operation x1 -> x0, local copies, waits for them, and re-layouts: 1.31 us -> none  [per_device(): router_weight[0].reshape(tile, part)]
where the time goes in v3:
time: 72 us; the launch traced here: 71.8 us
  Pallas kernels  66.5 us (92%)
  local copies, waits for them, and re-layouts  4.61 us (6%)
    pallas_call x1, Pallas kernels, per_device(): pl.pallas_call(functools.partial(kernel, groups, pipes, cap), out_shape=(...  66.5 us
    unnamed x4, local copies, waits for them, and re-layouts  4.61 us

profile of v3, /device:TPU:0, one launch (start us, length us, event | category | flops | bytes accessed | tf_op | source)
XLA Modules:
  0.0 71.8 jit_solution(2988789428946946826)
XLA Ops:
  0.6 66.5 %shard_map.86 = (bf16[2,512,1536]{2,1,0:T(8,128)(2,1)}, bf16[128,2048]{1,0:T(8,128)(2,1)}) custom-call(s32[8,128]{1,0:T(8,128)} %bitcast.21, s32[8,128]{1,0:T(8,128)} %bitcast.22, f32[8,128]{1,0:T(8,128)} %bitcast.23, bf16[128,2048]{1,0:T(8,128)(2,1)} %bitcast.19, bf16[2,2048]{1,0:T(2,128)(2,1)} %bitcast.20, bf16[2,512,1536]{2,1,0:T(8,128)(2,1)} %bitcast.18, ...), custom_call_target="tpu_custom_call" | custom-call | flops 3221225472 | bytes 16777216 | tf_op jit(solution)/shard_map/pallas_call | solution.py:388
  67.1 0.0 copy-start
  67.1 3.8 %copy.11 = bf16[1,2,512,1536]{3,2,1,0:T(8,128)(2,1)} copy(bf16[1,2,512,1536]{3,2,1,0:T(8,128)(2,1)} %bitcast.15) | data formatting | bytes 6291456
  71.0 0.0 copy-done
  71.0 0.8 %copy.12 = bf16[1,128,2048]{2,1,0:T(8,128)(2,1)} copy(bf16[1,128,2048]{2,1,0:T(8,128)(2,1)S(1)} %bitcast.16) | data formatting | bytes 1048576
Async XLA Ops:
  67.1 3.8 %copy-start = (bf16[128,2048]{1,0:T(8,128)(2,1)S(1)}, bf16[128,2048]{1,0:T(8,128)(2,1)}, u32[]{:S(2)}) copy-start(bf16[128,2048]{1,0:T(8,128)(2,1)} %get-tuple-element.5) | copy-start | bytes 1572868
